TPU v7x, 32 devices: a whole 2x2x4 slice. The times are simulated.
32 devices in a mesh: groups: 2 (over y), outer: 2 (over core), inner: 8 (over z, x).
Axes of the slice: x: 2, y: 2, z: 4, core: 2. Of those that a mesh axis runs over, the one named last changes fastest.
Arguments:
- queries: bfloat16 [8192, 2048], P(('groups', 'outer', 'inner')), parts along dimension 0, may hold values from -120 to 120
- key_value: bfloat16 [2, 8192, 2048], P(None, ('groups', 'outer', 'inner')), parts along dimension 1, may hold values from -6 to 6
- region_table: int32 [16, 8], P('groups'), parts along dimension 0, may hold values from 0 to 15, as said below
- region_bias: float32 [16, 16], replicated, may hold values from -4 to 4
Outputs:
- attended: bfloat16 [8192, 2048], P(('groups', 'outer', 'inner')), parts along dimension 0
There are 2 independent parts, one for each index of `groups`. A program takes and returns all parts, laid end to end along the dimension named above; an argument that names none is the same for every part. Nothing has to cross between parts.
Inputs may be any that keep to these rules, and one draw needn't show every extreme that they name: region_table[i, j] is 0 whenever |i - j| > 1, and region_table[i, i] >= 1.
All inputs are finite; a program needn't handle non-finite values.
Results may differ from a plain program's by a relative error of at most 0.0046.
Values may be sent and summed in bfloat16 or wider, within the bound.
A program may use at most 128 MiB of HBM per device.

v0:
```python
import math

import jax
import jax.numpy as jnp
from jax import lax
from jax.sharding import PartitionSpec as P


def from_behind(value, axis, steps):
    count = lax.axis_size(axis)
    leading, last = (max(0, -steps), min(count, count - steps))
    return lax.ppermute(value, axis, [(source, source + steps) for source in range(leading, last)])


def tile_scores(query_part, key_part, bias_part, live_flag, score_scale):
    products = jnp.einsum("thd,uhd->htu", query_part, key_part, preferred_element_type=jnp.float32)
    return jnp.where(live_flag, products * score_scale + bias_part[:, None, None], -1e30)


def tile_values(rounded, value_part):
    return jnp.einsum("htu,uhd->thd", rounded, value_part, preferred_element_type=jnp.float32)


def per_device(queries, key_value, region_table, region_bias):
    tokens, feature_width = queries.shape
    head_count = region_bias.shape[0]
    head_size = feature_width // head_count
    head_group = math.gcd(4, head_count)
    column_span = head_group * head_size
    devices = lax.axis_size(("outer", "inner"))
    device_index = lax.axis_index(("outer", "inner"))
    query_block = device_index // 2
    pieces = []
    key_blocks = []
    in_ranges = []
    lower_pieces = {}
    upper_pieces = {}
    for distance in (1, 2, 3):
        lower_pieces[distance] = from_behind(key_value, ("outer", "inner"), distance)
        upper_pieces[distance] = from_behind(key_value, ("outer", "inner"), -distance)
    ordered = [
        lower_pieces[3],
        lower_pieces[2],
        lower_pieces[1],
        key_value,
        upper_pieces[1],
        upper_pieces[2],
        upper_pieces[3],
    ]
    for offset, key_piece in zip((-3, -2, -1, 0, 1, 2, 3), ordered):
        source = device_index + offset
        pieces.append(key_piece)
        in_ranges.append((source >= 0) & (source < devices))
        key_blocks.append(jnp.clip(source, 0, devices - 1) // 2)
    regions = jnp.arange(region_bias.shape[1], dtype=jnp.int32)
    live_flags = []
    biases = []
    for in_range, key_block in zip(in_ranges, key_blocks):
        region = region_table[query_block, key_block]
        live_flags.append(in_range & (region > 0))
        biases.append(jnp.sum(jnp.where(regions[None, :] == region, region_bias, 0.0), axis=1))
    score_scale = 1.0 / math.sqrt(head_size)

    def attend(group_index, result):
        column_start = group_index * column_span
        query_part = lax.dynamic_slice_in_dim(queries, column_start, column_span, 1).reshape(
            tokens, head_group, head_size
        )
        value_parts = []
        scores = []
        for key_piece, live_flag, bias_row in zip(pieces, live_flags, biases):
            key_length = key_piece.shape[1]
            key_part = lax.dynamic_slice_in_dim(key_piece[0], column_start, column_span, 1).reshape(
                key_length, head_group, head_size
            )
            value_part = lax.dynamic_slice_in_dim(
                key_piece[1], column_start, column_span, 1
            ).reshape(key_length, head_group, head_size)
            bias_part = lax.dynamic_slice_in_dim(bias_row, group_index * head_group, head_group, 0)
            value_parts.append(value_part)
            tile = tile_scores(query_part, key_part, bias_part, live_flag, score_scale)
            scores.append(tile)
        row_peak = jnp.max(jnp.stack([jnp.max(tile, axis=-1) for tile in scores]), axis=0)
        row_total = jnp.zeros((head_group, tokens), jnp.float32)
        weighted = jnp.zeros((tokens, head_group, head_size), jnp.float32)
        for tile, value_part, live_flag in zip(scores, value_parts, live_flags):
            weights = jnp.exp(tile - row_peak[:, :, None])
            row_total = row_total + jnp.sum(weights, axis=-1)
            rounded = weights.astype(jnp.bfloat16)
            weighted = weighted + tile_values(rounded, value_part)
        attended = (
            (weighted / row_total.T[:, :, None]).reshape(tokens, column_span).astype(jnp.bfloat16)
        )
        return lax.dynamic_update_slice_in_dim(result, attended, column_start, 1)

    return lax.fori_loop(
        0, head_count // head_group, attend, jnp.zeros((tokens, feature_width), jnp.bfloat16)
    )


def solution(mesh):
    placed = (
        P(("groups", "outer", "inner"), None),
        P(None, ("groups", "outer", "inner"), None),
        P("groups", None),
        P(),
    )
    return jax.shard_map(
        per_device,
        mesh=mesh,
        in_specs=placed,
        out_specs=P(("groups", "outer", "inner"), None),
        check_vma=False,
    )
```

profile of v0, /device:TPU:14, one launch (start us, length us, event | category | flops | bytes accessed | tf_op | source)
XLA Modules:
  0.0 314.4 jit_solution(6898019181190784521)
XLA Ops:
  0.0 2.9 copy.41
  2.9 2.3 collective-permute-start.5
  5.2 1.9 collective-permute-start.4
  7.2 1.9 collective-permute-start.3
  9.1 4.8 %collective-permute-start.2 = (bf16[2,256,2048]{1,2,0:T(8,128)(2,1)S(1)}, bf16[2,256,2048]{1,2,0:T(8,128)(2,1)}, u32[]{:S(2)}, u32[]{:S(2)}) collective-permute-start(bf16[2,256,2048]{1,2,0:T(8,128)(2,1)S(1)} %copy.41), channel_id=1, source_target_pairs={{0,1},{1,2},{2,3},{3,4},{4,5},{5,6},{6,7},{7,8},{8,9},{9,10},{10,1... | collective-permute-start | bytes 6291464 | tf_op jit(solution)/shard_map/ppermute | solution.py:12
  13.9 3.9 %collective-permute-start.1 = (bf16[2,256,2048]{1,2,0:T(8,128)(2,1)S(1)}, bf16[2,256,2048]{1,2,0:T(8,128)(2,1)}, u32[]{:S(2)}, u32[]{:S(2)}) collective-permute-start(bf16[2,256,2048]{1,2,0:T(8,128)(2,1)S(1)} %copy.41), channel_id=1, source_target_pairs={{0,2},{1,3},{2,4},{3,5},{4,6},{5,7},{6,8},{7,9},{8,10},{9,11},{10,... | collective-permute-start | bytes 6291464 | tf_op jit(solution)/shard_map/ppermute | solution.py:12
  17.8 37.3 %collective-permute-done.5 = bf16[2,256,2048]{1,2,0:T(8,128)(2,1)S(1)} collective-permute-done((bf16[2,256,2048]{1,2,0:T(8,128)(2,1)S(1)}, bf16[2,256,2048]{1,2,0:T(8,128)(2,1)S(1)}, u32[]{:S(2)}, u32[]{:S(2)}) %collective-permute-start.5) | collective-permute-done | bytes 2097184 | tf_op jit(solution)/shard_map/ppermute | solution.py:12
  55.1 1.3 copy-done
  56.4 1.9 collective-permute-start
  64.1 1.3 iota_compare_fusion
  65.3 1.2 iota_compare_fusion.2
  66.5 1.2 iota_compare_fusion.4
  68.0 51.7 %collective-permute-done.4 = bf16[2,256,2048]{1,2,0:T(8,128)(2,1)} collective-permute-done((bf16[2,256,2048]{1,2,0:T(8,128)(2,1)S(1)}, bf16[2,256,2048]{1,2,0:T(8,128)(2,1)}, u32[]{:S(2)}, u32[]{:S(2)}) %collective-permute-start.4) | collective-permute-done | bytes 2097184 | tf_op jit(solution)/shard_map/ppermute | solution.py:12
  119.7 121.4 %collective-permute-done.3 = bf16[2,256,2048]{1,2,0:T(8,128)(2,1)} collective-permute-done((bf16[2,256,2048]{1,2,0:T(8,128)(2,1)S(1)}, bf16[2,256,2048]{1,2,0:T(8,128)(2,1)}, u32[]{:S(2)}, u32[]{:S(2)}) %collective-permute-start.3) | collective-permute-done | bytes 2097184 | tf_op jit(solution)/shard_map/ppermute | solution.py:12
  242.2 72.2 %while.13 = (s32[]{:T(128)}, bf16[256,2048]{1,0:T(8,128)(2,1)}, bf16[2,256,2048]{1,2,0:T(8,128)(2,1)}, pred[]{:T(512)}, bf16[256,2048]{1,0:T(8,128)(2,1)}, /*ind...) while((s32[]{:T(128)}, bf16[256,2048]{1,0:T(8,128)(2,1)}, ...), condition=%wide.region_22.23_spmd, body=%wide.region_7.22_spmd.sunk | while | flops 955250688 | bytes 81425192 | solution.py:96
  243.8 1.7 fusion.152
  246.0 1.1 copy-done.1
  247.1 1.8 fusion.154
  249.8 1.8 fusion.157
  252.6 2.4 fusion.160
  261.9 1.7 fusion.152
  265.2 1.8 fusion.154
  267.9 1.8 fusion.157
  270.6 2.4 fusion.160
  279.9 1.7 fusion.152
  283.2 1.8 fusion.154
  285.9 1.8 fusion.157
  288.7 2.4 fusion.160
  298.0 1.7 fusion.152
  301.3 1.8 fusion.154
  304.0 1.8 fusion.157
  306.7 2.4 fusion.160
  (183 shorter events, 41.7 us)
Async XLA Ops:
  0.0 58.5 %copy-start.3 = (s32[8,8]{1,0:T(8,128)S(1)}, s32[8,8]{1,0:T(8,128)}, u32[]{:S(2)}) copy-start(s32[8,8]{1,0:T(8,128)} %param.8) | copy-start | bytes 772
  0.0 67.7 %copy-start.2 = (f32[16,16]{1,0:T(8,128)S(1)}, f32[16,16]{1,0:T(8,128)}, u32[]{:S(2)}) copy-start(f32[16,16]{1,0:T(8,128)} %param.9) | copy-start | bytes 3076
  2.9 52.3 %collective-permute-start.5 = (bf16[2,256,2048]{1,2,0:T(8,128)(2,1)S(1)}, bf16[2,256,2048]{1,2,0:T(8,128)(2,1)S(1)}, u32[]{:S(2)}, u32[]{:S(2)}) collective-permute-start(bf16[2,256,2048]{1,2,0:T(8,128)(2,1)S(1)} %copy.41), channel_id=1, source_target_pairs={{3,0},{4,1},{5,2},{6,3},{7,4},{8,5},{9,6},{10,7},{11,8},{12,9},{13... | collective-permute-start | bytes 6291464 | tf_op jit(solution)/shard_map/ppermute | solution.py:12
  5.2 114.5 %collective-permute-start.4 = (bf16[2,256,2048]{1,2,0:T(8,128)(2,1)S(1)}, bf16[2,256,2048]{1,2,0:T(8,128)(2,1)}, u32[]{:S(2)}, u32[]{:S(2)}) collective-permute-start(bf16[2,256,2048]{1,2,0:T(8,128)(2,1)S(1)} %copy.41), channel_id=1, source_target_pairs={{2,0},{3,1},{4,2},{5,3},{6,4},{7,5},{8,6},{9,7},{10,8},{11,9},{12,... | collective-permute-start | bytes 6291464 | tf_op jit(solution)/shard_map/ppermute | solution.py:12
  7.2 234.0 %collective-permute-start.3 = (bf16[2,256,2048]{1,2,0:T(8,128)(2,1)S(1)}, bf16[2,256,2048]{1,2,0:T(8,128)(2,1)}, u32[]{:S(2)}, u32[]{:S(2)}) collective-permute-start(bf16[2,256,2048]{1,2,0:T(8,128)(2,1)S(1)} %copy.41), channel_id=1, source_target_pairs={{1,0},{2,1},{3,2},{4,3},{5,4},{6,5},{7,6},{8,7},{9,8},{10,9},{11,1... | collective-permute-start | bytes 6291464 | tf_op jit(solution)/shard_map/ppermute | solution.py:12
  9.1 232.0 %collective-permute-start.2 = (bf16[2,256,2048]{1,2,0:T(8,128)(2,1)S(1)}, bf16[2,256,2048]{1,2,0:T(8,128)(2,1)}, u32[]{:S(2)}, u32[]{:S(2)}) collective-permute-start(bf16[2,256,2048]{1,2,0:T(8,128)(2,1)S(1)} %copy.41), channel_id=1, source_target_pairs={{0,1},{1,2},{2,3},{3,4},{4,5},{5,6},{6,7},{7,8},{8,9},{9,10},{10,1... | collective-permute-start | bytes 6291464 | tf_op jit(solution)/shard_map/ppermute | solution.py:12
  13.9 227.2 %collective-permute-start.1 = (bf16[2,256,2048]{1,2,0:T(8,128)(2,1)S(1)}, bf16[2,256,2048]{1,2,0:T(8,128)(2,1)}, u32[]{:S(2)}, u32[]{:S(2)}) collective-permute-start(bf16[2,256,2048]{1,2,0:T(8,128)(2,1)S(1)} %copy.41), channel_id=1, source_target_pairs={{0,2},{1,3},{2,4},{3,5},{4,6},{5,7},{6,8},{7,9},{8,10},{9,11},{10,... | collective-permute-start | bytes 6291464 | tf_op jit(solution)/shard_map/ppermute | solution.py:12
  55.1 1.3 copy-start
  56.4 184.7 %collective-permute-start = (bf16[2,256,2048]{1,2,0:T(8,128)(2,1)S(1)}, bf16[2,256,2048]{1,2,0:T(8,128)(2,1)}, u32[]{:S(2)}, u32[]{:S(2)}) collective-permute-start(bf16[2,256,2048]{1,2,0:T(8,128)(2,1)S(1)} %copy.41), channel_id=1, source_target_pairs={{0,3},{1,4},{2,5},{3,6},{4,7},{5,8},{6,9},{7,10},{8,11},{9,12},{10... | collective-permute-start | bytes 6291464 | tf_op jit(solution)/shard_map/ppermute | solution.py:12
  245.5 1.6 copy-start.1
  263.6 1.6 copy-start.1
  281.6 1.6 copy-start.1
  299.7 1.6 copy-start.1
where the time goes:
time: 315 us; the launch traced here: 314 us
  waiting for transfers between devices  210 us (67%)
  local copies, waits for them, and re-layouts  52.9 us (17%)
  matrix products  19.6 us (6%)
  starting transfers between devices  16.8 us (5%)
  other arithmetic  9.11 us (3%)
  between operations  4.52 us (1%)
    ppermute x6, waiting for transfers between devices, from_behind(): lax.ppermute(value, axis, [(source, source + steps) for source in range(l...  210 us
    slice x12, local copies, waits for them, and re-layouts, attend(): key_piece[1]  24.3 us
    ppermute x6, starting transfers between devices, from_behind(): lax.ppermute(value, axis, [(source, source + steps) for source in range(l...  16.8 us
    dot_general x28, matrix products, tile_scores(): jnp.einsum('thd,uhd->htu', query_part, key_part, preferred_element_type=j...  10.6 us
    dot_general x28, matrix products, tile_values(): jnp.einsum('htu,uhd->thd', rounded, value_part, preferred_element_type=jn...  9 us
    slice x4, local copies, waits for them, and re-layouts, attend(): key_piece[0]  6.71 us
  transfers between devices with their start and end apart: 6, of which 3 were waited for; matrix products, arithmetic and copies ran while one was open for 2% of the time, Pallas kernels for 0%

commit v1 on v0

v1 whole, which is shorter than its diff:
```python
import functools
import math

import jax
import jax.numpy as jnp
from jax import lax
from jax.experimental import pallas as pl
from jax.experimental.pallas import tpu as pltpu
from jax.sharding import PartitionSpec as P

MESH = pl.DeviceIdType.MESH
BELOW, OWN, ABOVE = 0, 1, 2
LOG2E = math.log2(math.e)
DEAD = -1e30


def kernel(
    inner,
    positions,
    table_ref,
    bias_ref,
    q_ref,
    kv_ref,
    out_ref,
    q_buf,
    kv_buf,
    o_buf,
    q_local,
    kv_local,
    o_local,
    q_send,
    q_recv,
    kv_send,
    kv_recv,
    z_send,
    z_recv,
    o_send,
    o_recv,
):
    heads, _, _, block, head_size = kv_buf.shape
    rows = block // 2
    group = lax.axis_index("groups")
    position = lax.axis_index("outer") * inner + lax.axis_index("inner")
    side = lax.rem(position, 2)
    has_below = position >= 2
    has_above = position < positions - 2

    def at(where):
        return (group, where // inner, lax.rem(where, inner))

    partner = at(position + 1 - 2 * side)
    below = at(jnp.maximum(position - 2, 0))
    above = at(jnp.minimum(position + 2, positions - 1))
    own_rows = pl.ds(pl.multiple_of(side * rows, rows), rows)
    partner_rows = pl.ds(pl.multiple_of((1 - side) * rows, rows), rows)

    def columns(which_side, head):
        return pl.ds(pl.multiple_of((which_side * heads + head) * head_size, head_size), head_size)

    def remote(src, dst, send, recv, target):
        return pltpu.make_async_remote_copy(
            src_ref=src, dst_ref=dst, send_sem=send, recv_sem=recv, device_id=target, device_id_type=MESH
        )

    def q_pair(head, which_rows):
        return remote(
            q_ref.at[:, columns(1 - side, head)],
            q_buf.at[head, which_rows],
            q_send.at[head],
            q_recv.at[head],
            partner,
        )

    def kv_pair(head, which_rows):
        return remote(
            kv_ref.at[:, :, columns(1 - side, head)],
            kv_buf.at[head, OWN, :, which_rows],
            kv_send.at[head],
            kv_recv.at[head],
            partner,
        )

    def q_keep(head):
        return pltpu.make_async_copy(
            q_ref.at[:, columns(side, head)], q_buf.at[head, own_rows], q_local.at[head]
        )

    def kv_keep(head):
        return pltpu.make_async_copy(
            kv_ref.at[:, :, columns(side, head)], kv_buf.at[head, OWN, :, own_rows], kv_local.at[head]
        )

    def own_along(head, up):
        return remote(
            kv_ref.at[:, :, columns(side, head)],
            kv_buf.at[head, BELOW if up else ABOVE, :, own_rows],
            z_send.at[int(up), 0, head],
            z_recv.at[int(up), 0, head],
            above if up else below,
        )

    def passed_along(head, up):
        return remote(
            kv_buf.at[head, OWN, :, partner_rows],
            kv_buf.at[head, BELOW if up else ABOVE, :, partner_rows],
            z_send.at[int(up), 1, head],
            z_recv.at[int(up), 1, head],
            above if up else below,
        )

    def out_pair(head, which_side):
        return remote(
            o_buf.at[head, partner_rows],
            out_ref.at[:, columns(which_side, head)],
            o_send.at[head],
            o_recv.at[head],
            partner,
        )

    def out_keep(head):
        return pltpu.make_async_copy(
            o_buf.at[head, own_rows], out_ref.at[:, columns(side, head)], o_local.at[head]
        )

    def each_head(body):
        lax.fori_loop(0, heads, lambda head, carry: (body(head), carry)[1], 0)

    barrier = pltpu.get_barrier_semaphore()
    pl.semaphore_signal(barrier, inc=1, device_id=partner, device_id_type=MESH)

    @pl.when(has_below)
    def _():
        pl.semaphore_signal(barrier, inc=1, device_id=below, device_id_type=MESH)

    @pl.when(has_above)
    def _():
        pl.semaphore_signal(barrier, inc=1, device_id=above, device_id_type=MESH)

    pl.semaphore_wait(barrier, 1 + has_below.astype(jnp.int32) + has_above.astype(jnp.int32))

    def start_first(head):
        kv_pair(head, own_rows).start()

        @pl.when(has_above)
        def _():
            own_along(head, True).start()

        @pl.when(has_below)
        def _():
            own_along(head, False).start()

    each_head(start_first)

    def start_second(head):
        q_pair(head, own_rows).start()
        q_keep(head).start()
        kv_keep(head).start()

    each_head(start_second)

    @pl.when(jnp.logical_not(has_below))
    def _():
        each_head(lambda head: kv_buf.__setitem__((head, BELOW), jnp.zeros((2, block, head_size), kv_buf.dtype)))

    @pl.when(jnp.logical_not(has_above))
    def _():
        each_head(lambda head: kv_buf.__setitem__((head, ABOVE), jnp.zeros((2, block, head_size), kv_buf.dtype)))

    def pass_on(head):
        kv_pair(head, partner_rows).wait_recv()

        @pl.when(has_above)
        def _():
            passed_along(head, True).start()

        @pl.when(has_below)
        def _():
            passed_along(head, False).start()

    each_head(pass_on)

    block_index = position // 2
    last_block = positions // 2 - 1
    scale = LOG2E / math.sqrt(head_size)

    def key_bias(head, slot):
        key_block = jnp.clip(block_index + slot - 1, 0, last_block)
        region = table_ref[block_index, key_block]
        live = region > 0
        if slot == BELOW:
            live = live & has_below
        if slot == ABOVE:
            live = live & has_above
        return jnp.where(live, bias_ref[side * heads + head, region] * LOG2E, DEAD)

    def attend(head):
        q_pair(head, partner_rows).wait_recv()
        q_keep(head).wait()
        kv_keep(head).wait()

        @pl.when(has_below)
        def _():
            own_along(head, True).wait_recv()
            passed_along(head, True).wait_recv()

        @pl.when(has_above)
        def _():
            own_along(head, False).wait_recv()
            passed_along(head, False).wait_recv()

        biases = [key_bias(head, slot) for slot in (BELOW, OWN, ABOVE)]
        for half in range(2):
            tile = pl.ds(half * rows, rows)
            query = q_buf[head, tile]
            products = [
                lax.dot_general(
                    query, kv_buf[head, slot, 0], (((1,), (1,)), ((), ())), preferred_element_type=jnp.float32
                )
                for slot in (BELOW, OWN, ABOVE)
            ]
            peak = functools.reduce(
                jnp.maximum,
                [jnp.max(tile_, axis=1, keepdims=True) * scale + bias for tile_, bias in zip(products, biases)],
            )
            total = jnp.zeros((rows, 1), jnp.float32)
            weighted = jnp.zeros((rows, head_size), jnp.float32)
            for slot in (BELOW, OWN, ABOVE):
                weights = jnp.exp2(products[slot] * scale + (biases[slot] - peak))
                total = total + jnp.sum(weights, axis=1, keepdims=True)
                weighted = weighted + jnp.dot(
                    weights.astype(jnp.bfloat16), kv_buf[head, slot, 1], preferred_element_type=jnp.float32
                )
            o_buf[head, tile] = (weighted / total).astype(o_buf.dtype)
        out_pair(head, side).start()
        out_keep(head).start()

    each_head(attend)

    def finish(head):
        out_keep(head).wait()
        out_pair(head, side).wait_send()
        out_pair(head, 1 - side).wait_recv()
        q_pair(head, own_rows).wait_send()
        kv_pair(head, own_rows).wait_send()

        @pl.when(has_above)
        def _():
            own_along(head, True).wait_send()
            passed_along(head, True).wait_send()

        @pl.when(has_below)
        def _():
            own_along(head, False).wait_send()
            passed_along(head, False).wait_send()

    each_head(finish)


def per_device(inner, positions, queries, key_value, region_table, region_bias):
    tokens, feature_width = queries.shape
    head_count = region_bias.shape[0]
    head_size = feature_width // head_count
    heads = head_count // 2
    block = 2 * tokens
    dma = pltpu.SemaphoreType.DMA
    return pl.pallas_call(
        functools.partial(kernel, inner, positions),
        out_shape=jax.ShapeDtypeStruct((tokens, feature_width), jnp.bfloat16),
        in_specs=[
            pl.BlockSpec(memory_space=pltpu.SMEM),
            pl.BlockSpec(memory_space=pltpu.SMEM),
            pl.BlockSpec(memory_space=pl.ANY),
            pl.BlockSpec(memory_space=pl.ANY),
        ],
        out_specs=pl.BlockSpec(memory_space=pl.ANY),
        scratch_shapes=[
            pltpu.VMEM((heads, block, head_size), jnp.bfloat16),
            pltpu.VMEM((heads, 3, 2, block, head_size), jnp.bfloat16),
            pltpu.VMEM((heads, block, head_size), jnp.bfloat16),
            dma((heads,)),
            dma((heads,)),
            dma((heads,)),
            dma((heads,)),
            dma((heads,)),
            dma((heads,)),
            dma((heads,)),
            dma((2, 2, heads)),
            dma((2, 2, heads)),
            dma((heads,)),
            dma((heads,)),
        ],
        compiler_params=pltpu.CompilerParams(
            collective_id=0, has_side_effects=True, vmem_limit_bytes=48 * 1024 * 1024
        ),
    )(region_table, region_bias, queries, key_value)


def solution(mesh):
    inner = mesh.shape["inner"]
    positions = mesh.shape["outer"] * inner
    placed = (
        P(("groups", "outer", "inner"), None),
        P(None, ("groups", "outer", "inner"), None),
        P("groups", None),
        P(),
    )
    return jax.shard_map(
        functools.partial(per_device, inner, positions),
        mesh=mesh,
        in_specs=placed,
        out_specs=P(("groups", "outer", "inner"), None),
        check_vma=False,
    )
```

time: 315 us -> 84.3 us (0.27)
  the two profiles are of different devices: /device:TPU:14 before, /device:TPU:1 now
where the time goes in v1:
time: 84.3 us; the launch traced here: 83.8 us
  Pallas kernels  78.6 us (93%)
  local copies, waits for them, and re-layouts  5.17 us (6%)
    pallas_call x1, Pallas kernels, per_device(): pl.pallas_call(functools.partial(kernel, inner, positions), out_shape=jax...  78.6 us
    unnamed x9, local copies, waits for them, and re-layouts  5.17 us

profile of v1, /device:TPU:1, one launch (start us, length us, event | category | flops | bytes accessed | tf_op | source)
XLA Modules:
  0.0 83.8 jit_solution(17750321177881626355)
XLA Ops:
  0.0 0.0 copy-start
  0.0 1.6 %copy-done = bf16[2,256,2048]{2,1,0:T(8,128)(2,1)S(1)} copy-done((bf16[2,256,2048]{2,1,0:T(8,128)(2,1)S(1)}, bf16[2,256,2048]{2,1,0:T(8,128)(2,1)}, u32[]{:S(2)}) %copy-start) | copy-done | bytes 2097176
  1.6 0.0 copy-start.1
  1.6 1.2 %copy-done.1 = bf16[256,2048]{1,0:T(8,128)(2,1)S(1)} copy-done((bf16[256,2048]{1,0:T(8,128)(2,1)S(1)}, bf16[256,2048]{1,0:T(8,128)(2,1)}, u32[]{:S(2)}) %copy-start.1) | copy-done | bytes 1048600
  2.8 0.0 copy-start.2
  2.8 0.7 copy-done.2
  3.5 0.0 copy-start.3
  3.5 0.7 copy-done.3
  4.2 78.6 %shard_map.46 = bf16[256,2048]{1,0:T(8,128)(2,1)S(1)} custom-call(s32[8,8]{1,0:T(8,128)S(1)} %copy-done.3, f32[16,16]{1,0:T(8,128)S(1)} %copy-done.2, bf16[256,2048]{1,0:T(8,128)(2,1)S(1)} %copy-done.1, bf16[2,256,2048]{2,1,0:T(8,128)(2,1)S(1)} %copy-done), custom_call_target="tpu_custom_call" | custom-call | tf_op jit(solution)/shard_map/pallas_call | solution.py:266
  82.8 1.0 %copy.6 = bf16[256,2048]{1,0:T(8,128)(2,1)} copy(bf16[256,2048]{1,0:T(8,128)(2,1)S(1)} %shard_map.46) | data formatting | bytes 2097152
Async XLA Ops:
  0.0 1.6 %copy-start = (bf16[2,256,2048]{2,1,0:T(8,128)(2,1)S(1)}, bf16[2,256,2048]{2,1,0:T(8,128)(2,1)}, u32[]{:S(2)}) copy-start(bf16[2,256,2048]{2,1,0:T(8,128)(2,1)} %kv_ref.1) | copy-start | bytes 6291460
  1.6 1.2 %copy-start.1 = (bf16[256,2048]{1,0:T(8,128)(2,1)S(1)}, bf16[256,2048]{1,0:T(8,128)(2,1)}, u32[]{:S(2)}) copy-start(bf16[256,2048]{1,0:T(8,128)(2,1)} %q_ref.1) | copy-start | bytes 3145732
  2.8 0.7 copy-start.2
  3.5 0.7 copy-start.3

commit v2 on v1

--- a/solution.py
+++ b/solution.py
@@ -12,19 +12,25 @@
 BELOW, OWN, ABOVE = 0, 1, 2
 LOG2E = math.log2(math.e)
 DEAD = -1e30
+ALONG_AHEAD = 2
+PAIR_AHEAD = 4
 
 
 def kernel(
     inner,
     positions,
-    table_ref,
-    bias_ref,
+    table_hbm,
+    bias_hbm,
     q_ref,
     kv_ref,
     out_ref,
+    table_ref,
+    bias_ref,
     q_buf,
     kv_buf,
     o_buf,
+    table_local,
+    bias_local,
     q_local,
     kv_local,
     o_local,
@@ -125,6 +131,11 @@
     def each_head(body):
         lax.fori_loop(0, heads, lambda head, carry: (body(head), carry)[1], 0)
 
+    table_keep = pltpu.make_async_copy(table_hbm, table_ref, table_local)
+    bias_keep = pltpu.make_async_copy(bias_hbm, bias_ref, bias_local)
+    table_keep.start()
+    bias_keep.start()
+
     barrier = pltpu.get_barrier_semaphore()
     pl.semaphore_signal(barrier, inc=1, device_id=partner, device_id_type=MESH)
 
@@ -138,9 +149,11 @@
 
     pl.semaphore_wait(barrier, 1 + has_below.astype(jnp.int32) + has_above.astype(jnp.int32))
 
-    def start_first(head):
+    def start_pair(head):
         kv_pair(head, own_rows).start()
-
+        q_pair(head, own_rows).start()
+
+    def start_own(head):
         @pl.when(has_above)
         def _():
             own_along(head, True).start()
@@ -149,14 +162,26 @@
         def _():
             own_along(head, False).start()
 
-    each_head(start_first)
-
-    def start_second(head):
-        q_pair(head, own_rows).start()
+    def start_passed(head):
+        kv_pair(head, partner_rows).wait_recv()
+
+        @pl.when(has_above)
+        def _():
+            passed_along(head, True).start()
+
+        @pl.when(has_below)
+        def _():
+            passed_along(head, False).start()
+
+    def start_keep(head):
         q_keep(head).start()
         kv_keep(head).start()
 
-    each_head(start_second)
+    for head in range(PAIR_AHEAD):
+        start_pair(head)
+        if head < ALONG_AHEAD:
+            start_own(head)
+    each_head(start_keep)
 
     @pl.when(jnp.logical_not(has_below))
     def _():
@@ -166,18 +191,10 @@
     def _():
         each_head(lambda head: kv_buf.__setitem__((head, ABOVE), jnp.zeros((2, block, head_size), kv_buf.dtype)))
 
-    def pass_on(head):
-        kv_pair(head, partner_rows).wait_recv()
-
-        @pl.when(has_above)
-        def _():
-            passed_along(head, True).start()
-
-        @pl.when(has_below)
-        def _():
-            passed_along(head, False).start()
-
-    each_head(pass_on)
+    for head in range(ALONG_AHEAD):
+        start_passed(head)
+    table_keep.wait()
+    bias_keep.wait()
 
     block_index = position // 2
     last_block = positions // 2 - 1
@@ -207,6 +224,15 @@
         def _():
             own_along(head, False).wait_recv()
             passed_along(head, False).wait_recv()
+
+        @pl.when(head + ALONG_AHEAD < heads)
+        def _():
+            start_own(head + ALONG_AHEAD)
+            start_passed(head + ALONG_AHEAD)
+
+        @pl.when(head + PAIR_AHEAD < heads)
+        def _():
+            start_pair(head + PAIR_AHEAD)
 
         biases = [key_bias(head, slot) for slot in (BELOW, OWN, ABOVE)]
         for half in range(2):
@@ -267,16 +293,20 @@
         functools.partial(kernel, inner, positions),
         out_shape=jax.ShapeDtypeStruct((tokens, feature_width), jnp.bfloat16),
         in_specs=[
-            pl.BlockSpec(memory_space=pltpu.SMEM),
-            pl.BlockSpec(memory_space=pltpu.SMEM),
+            pl.BlockSpec(memory_space=pl.ANY),
+            pl.BlockSpec(memory_space=pl.ANY),
             pl.BlockSpec(memory_space=pl.ANY),
             pl.BlockSpec(memory_space=pl.ANY),
         ],
         out_specs=pl.BlockSpec(memory_space=pl.ANY),
         scratch_shapes=[
+            pltpu.SMEM(region_table.shape, region_table.dtype),
+            pltpu.SMEM(region_bias.shape, region_bias.dtype),
             pltpu.VMEM((heads, block, head_size), jnp.bfloat16),
             pltpu.VMEM((heads, 3, 2, block, head_size), jnp.bfloat16),
             pltpu.VMEM((heads, block, head_size), jnp.bfloat16),
+            dma,
+            dma,
             dma((heads,)),
             dma((heads,)),
             dma((heads,)),
@@ -290,7 +320,7 @@
             dma((heads,)),
         ],
         compiler_params=pltpu.CompilerParams(
-            collective_id=0, has_side_effects=True, vmem_limit_bytes=48 * 1024 * 1024
+            collective_id=0, has_side_effects=True, vmem_limit_bytes=60 * 1024 * 1024
         ),
     )(region_table, region_bias, queries, key_value)
 

time: 84.3 us -> 80.4 us (0.954)
  local copies, waits for them, and re-layouts: 5.17 us -> 2.3 us
    unnamed x9 -> x1, local copies, waits for them, and re-layouts: 5.17 us -> 2.3 us
where the time goes in v2:
time: 80.4 us; the launch traced here: 80.2 us
  Pallas kernels  77.9 us (97%)
  local copies, waits for them, and re-layouts  2.3 us (3%)
    pallas_call x1, Pallas kernels, per_device(): pl.pallas_call(functools.partial(kernel, inner, positions), out_shape=jax...  77.9 us
    unnamed x1, local copies, waits for them, and re-layouts  2.3 us

profile of v2, /device:TPU:1, one launch (start us, length us, event | category | flops | bytes accessed | tf_op | source)
XLA Modules:
  0.0 80.2 jit_solution(1589186854600907794)
XLA Ops:
  0.0 77.9 %shard_map.46 = bf16[256,2048]{1,0:T(8,128)(2,1)} custom-call(s32[8,8]{1,0:T(8,128)} %table_hbm.1, f32[16,16]{1,0:T(8,128)} %bias_hbm.1, bf16[256,2048]{1,0:T(8,128)(2,1)} %q_ref.1, bf16[2,256,2048]{2,1,0:T(8,128)(2,1)} %kv_ref.1), custom_call_target="tpu_custom_call" | custom-call | tf_op jit(solution)/shard_map/pallas_call | solution.py:292
  77.9 2.3 %copy.6 = bf16[256,2048]{1,0:T(8,128)(2,1)} copy(bf16[256,2048]{1,0:T(8,128)(2,1)} %shard_map.46) | data formatting | bytes 2097152

commit v3 on v2

--- a/solution.py
+++ b/solution.py
@@ -29,6 +29,7 @@
     q_buf,
     kv_buf,
     o_buf,
+    w_buf,
     table_local,
     bias_local,
     q_local,
@@ -96,23 +97,43 @@
             kv_ref.at[:, :, columns(side, head)], kv_buf.at[head, OWN, :, own_rows], kv_local.at[head]
         )
 
-    def own_along(head, up):
-        return remote(
-            kv_ref.at[:, :, columns(side, head)],
-            kv_buf.at[head, BELOW if up else ABOVE, :, own_rows],
-            z_send.at[int(up), 0, head],
-            z_recv.at[int(up), 0, head],
+    def own_along(head, part, up):
+        return remote(
+            kv_ref.at[part, :, columns(side, head)],
+            kv_buf.at[head, BELOW if up else ABOVE, part, own_rows],
+            z_send.at[int(up), 0, part, head],
+            z_recv.at[int(up), 0, part, head],
             above if up else below,
         )
 
-    def passed_along(head, up):
-        return remote(
-            kv_buf.at[head, OWN, :, partner_rows],
-            kv_buf.at[head, BELOW if up else ABOVE, :, partner_rows],
-            z_send.at[int(up), 1, head],
-            z_recv.at[int(up), 1, head],
+    def passed_along(head, part, up):
+        return remote(
+            kv_buf.at[head, OWN, part, partner_rows],
+            kv_buf.at[head, BELOW if up else ABOVE, part, partner_rows],
+            z_send.at[int(up), 1, part, head],
+            z_recv.at[int(up), 1, part, head],
             above if up else below,
         )
+
+    def both_ways(act):
+        @pl.when(has_above)
+        def _():
+            act(True)
+
+        @pl.when(has_below)
+        def _():
+            act(False)
+
+    def wait_along(head, part):
+        @pl.when(has_below)
+        def _():
+            own_along(head, part, True).wait_recv()
+            passed_along(head, part, True).wait_recv()
+
+        @pl.when(has_above)
+        def _():
+            own_along(head, part, False).wait_recv()
+            passed_along(head, part, False).wait_recv()
 
     def out_pair(head, which_side):
         return remote(
@@ -131,21 +152,27 @@
     def each_head(body):
         lax.fori_loop(0, heads, lambda head, carry: (body(head), carry)[1], 0)
 
+    barrier = pltpu.get_barrier_semaphore()
+    pl.semaphore_signal(barrier, inc=1, device_id=partner, device_id_type=MESH)
+
+    @pl.when(has_below)
+    def _():
+        pl.semaphore_signal(barrier, inc=1, device_id=below, device_id_type=MESH)
+
+    @pl.when(has_above)
+    def _():
+        pl.semaphore_signal(barrier, inc=1, device_id=above, device_id_type=MESH)
+
     table_keep = pltpu.make_async_copy(table_hbm, table_ref, table_local)
     bias_keep = pltpu.make_async_copy(bias_hbm, bias_ref, bias_local)
     table_keep.start()
     bias_keep.start()
 
-    barrier = pltpu.get_barrier_semaphore()
-    pl.semaphore_signal(barrier, inc=1, device_id=partner, device_id_type=MESH)
-
-    @pl.when(has_below)
-    def _():
-        pl.semaphore_signal(barrier, inc=1, device_id=below, device_id_type=MESH)
-
-    @pl.when(has_above)
-    def _():
-        pl.semaphore_signal(barrier, inc=1, device_id=above, device_id_type=MESH)
+    def start_keep(head):
+        q_keep(head).start()
+        kv_keep(head).start()
+
+    each_head(start_keep)
 
     pl.semaphore_wait(barrier, 1 + has_below.astype(jnp.int32) + has_above.astype(jnp.int32))
 
@@ -153,35 +180,18 @@
         kv_pair(head, own_rows).start()
         q_pair(head, own_rows).start()
 
-    def start_own(head):
-        @pl.when(has_above)
-        def _():
-            own_along(head, True).start()
-
-        @pl.when(has_below)
-        def _():
-            own_along(head, False).start()
-
-    def start_passed(head):
-        kv_pair(head, partner_rows).wait_recv()
-
-        @pl.when(has_above)
-        def _():
-            passed_along(head, True).start()
-
-        @pl.when(has_below)
-        def _():
-            passed_along(head, False).start()
-
-    def start_keep(head):
-        q_keep(head).start()
-        kv_keep(head).start()
-
-    for head in range(PAIR_AHEAD):
+    def start_own(head, part):
+        both_ways(lambda up: own_along(head, part, up).start())
+
+    def start_passed(head, part):
+        both_ways(lambda up: passed_along(head, part, up).start())
+
+    for head in range(ALONG_AHEAD):
+        start_own(head, 0)
         start_pair(head)
-        if head < ALONG_AHEAD:
-            start_own(head)
-    each_head(start_keep)
+        start_own(head, 1)
+    for head in range(ALONG_AHEAD, PAIR_AHEAD):
+        start_pair(head)
 
     @pl.when(jnp.logical_not(has_below))
     def _():
@@ -192,7 +202,9 @@
         each_head(lambda head: kv_buf.__setitem__((head, ABOVE), jnp.zeros((2, block, head_size), kv_buf.dtype)))
 
     for head in range(ALONG_AHEAD):
-        start_passed(head)
+        kv_pair(head, partner_rows).wait_recv()
+        start_passed(head, 0)
+        start_passed(head, 1)
     table_keep.wait()
     bias_keep.wait()
 
@@ -214,70 +226,68 @@
         q_pair(head, partner_rows).wait_recv()
         q_keep(head).wait()
         kv_keep(head).wait()
-
-        @pl.when(has_below)
-        def _():
-            own_along(head, True).wait_recv()
-            passed_along(head, True).wait_recv()
-
-        @pl.when(has_above)
-        def _():
-            own_along(head, False).wait_recv()
-            passed_along(head, False).wait_recv()
+        wait_along(head, 0)
 
         @pl.when(head + ALONG_AHEAD < heads)
         def _():
-            start_own(head + ALONG_AHEAD)
-            start_passed(head + ALONG_AHEAD)
+            kv_pair(head + ALONG_AHEAD, partner_rows).wait_recv()
+            start_own(head + ALONG_AHEAD, 0)
+            start_passed(head + ALONG_AHEAD, 0)
+            start_own(head + ALONG_AHEAD, 1)
+            start_passed(head + ALONG_AHEAD, 1)
 
         @pl.when(head + PAIR_AHEAD < heads)
         def _():
             start_pair(head + PAIR_AHEAD)
 
-        biases = [key_bias(head, slot) for slot in (BELOW, OWN, ABOVE)]
-        for half in range(2):
-            tile = pl.ds(half * rows, rows)
+        slots = (BELOW, OWN, ABOVE)
+        biases = [key_bias(head, slot) for slot in slots]
+        totals = []
+        for half, tile in enumerate((partner_rows, own_rows)):
             query = q_buf[head, tile]
             products = [
                 lax.dot_general(
                     query, kv_buf[head, slot, 0], (((1,), (1,)), ((), ())), preferred_element_type=jnp.float32
                 )
-                for slot in (BELOW, OWN, ABOVE)
+                for slot in slots
             ]
             peak = functools.reduce(
                 jnp.maximum,
-                [jnp.max(tile_, axis=1, keepdims=True) * scale + bias for tile_, bias in zip(products, biases)],
+                [jnp.max(scores, axis=1, keepdims=True) * scale + bias for scores, bias in zip(products, biases)],
             )
             total = jnp.zeros((rows, 1), jnp.float32)
-            weighted = jnp.zeros((rows, head_size), jnp.float32)
-            for slot in (BELOW, OWN, ABOVE):
+            for slot in slots:
                 weights = jnp.exp2(products[slot] * scale + (biases[slot] - peak))
                 total = total + jnp.sum(weights, axis=1, keepdims=True)
+                w_buf[half, slot] = weights.astype(w_buf.dtype)
+            totals.append(total)
+        wait_along(head, 1)
+        for half, tile in enumerate((partner_rows, own_rows)):
+            weighted = jnp.zeros((rows, head_size), jnp.float32)
+            for slot in slots:
                 weighted = weighted + jnp.dot(
-                    weights.astype(jnp.bfloat16), kv_buf[head, slot, 1], preferred_element_type=jnp.float32
+                    w_buf[half, slot], kv_buf[head, slot, 1], preferred_element_type=jnp.float32
                 )
-            o_buf[head, tile] = (weighted / total).astype(o_buf.dtype)
-        out_pair(head, side).start()
+            o_buf[head, tile] = (weighted / totals[half]).astype(o_buf.dtype)
+            if half == 0:
+                out_pair(head, side).start()
         out_keep(head).start()
 
     each_head(attend)
+
+    def finish_sends(head):
+        q_pair(head, own_rows).wait_send()
+        kv_pair(head, own_rows).wait_send()
+        for part in range(2):
+            both_ways(lambda up: own_along(head, part, up).wait_send())
+            both_ways(lambda up: passed_along(head, part, up).wait_send())
+
+    each_head(finish_sends)
 
     def finish(head):
         out_keep(head).wait()
         out_pair(head, side).wait_send()
         out_pair(head, 1 - side).wait_recv()
-        q_pair(head, own_rows).wait_send()
-        kv_pair(head, own_rows).wait_send()
-
-        @pl.when(has_above)
-        def _():
-            own_along(head, True).wait_send()
-            passed_along(head, True).wait_send()
-
-        @pl.when(has_below)
-        def _():
-            own_along(head, False).wait_send()
-            passed_along(head, False).wait_send()
 
     each_head(finish)
 
@@ -305,6 +315,7 @@
             pltpu.VMEM((heads, block, head_size), jnp.bfloat16),
             pltpu.VMEM((heads, 3, 2, block, head_size), jnp.bfloat16),
             pltpu.VMEM((heads, block, head_size), jnp.bfloat16),
+            pltpu.VMEM((2, 3, tokens, block), jnp.bfloat16),
             dma,
             dma,
             dma((heads,)),
@@ -314,8 +325,8 @@
             dma((heads,)),
             dma((heads,)),
             dma((heads,)),
-            dma((2, 2, heads)),
-            dma((2, 2, heads)),
+            dma((2, 2, 2, heads)),
+            dma((2, 2, 2, heads)),
             dma((heads,)),
             dma((heads,)),
         ],

time: 80.4 us -> 80 us (level)
  no operation moved by 1% of the time
where the time goes in v3:
time: 80 us; the launch traced here: 79.8 us
  Pallas kernels  77.5 us (97%)
  local copies, waits for them, and re-layouts  2.3 us (3%)
    pallas_call x1, Pallas kernels, per_device(): pl.pallas_call(functools.partial(kernel, inner, positions), out_shape=jax...  77.5 us
    unnamed x1, local copies, waits for them, and re-layouts  2.3 us

profile of v3, /device:TPU:1, one launch (start us, length us, event | category | flops | bytes accessed | tf_op | source)
XLA Modules:
  0.0 79.8 jit_solution(11721237637648415601)
XLA Ops:
  0.0 77.5 %shard_map.46 = bf16[256,2048]{1,0:T(8,128)(2,1)} custom-call(s32[8,8]{1,0:T(8,128)} %table_hbm.1, f32[16,16]{1,0:T(8,128)} %bias_hbm.1, bf16[256,2048]{1,0:T(8,128)(2,1)} %q_ref.1, bf16[2,256,2048]{2,1,0:T(8,128)(2,1)} %kv_ref.1), custom_call_target="tpu_custom_call" | custom-call | tf_op jit(solution)/shard_map/pallas_call | solution.py:302
  77.5 2.3 %copy.6 = bf16[256,2048]{1,0:T(8,128)(2,1)} copy(bf16[256,2048]{1,0:T(8,128)(2,1)} %shard_map.46) | data formatting | bytes 2097152

commit v4 on v3

--- a/solution.py
+++ b/solution.py
@@ -14,6 +14,7 @@
 DEAD = -1e30
 ALONG_AHEAD = 2
 PAIR_AHEAD = 4
+FINISH_BEHIND = 3
 
 
 def kernel(
@@ -222,6 +223,18 @@
             live = live & has_above
         return jnp.where(live, bias_ref[side * heads + head, region] * LOG2E, DEAD)
 
+    def finish_sends(head):
+        q_pair(head, own_rows).wait_send()
+        kv_pair(head, own_rows).wait_send()
+        for part in range(2):
+            both_ways(lambda up: own_along(head, part, up).wait_send())
+            both_ways(lambda up: passed_along(head, part, up).wait_send())
+
+    def finish(head):
+        out_keep(head).wait()
+        out_pair(head, side).wait_send()
+        out_pair(head, 1 - side).wait_recv()
+
     def attend(head):
         q_pair(head, partner_rows).wait_recv()
         q_keep(head).wait()
@@ -239,6 +252,11 @@
         @pl.when(head + PAIR_AHEAD < heads)
         def _():
             start_pair(head + PAIR_AHEAD)
+
+        @pl.when(head >= FINISH_BEHIND)
+        def _():
+            finish_sends(head - FINISH_BEHIND)
+            finish(head - FINISH_BEHIND)
 
         slots = (BELOW, OWN, ABOVE)
         biases = [key_bias(head, slot) for slot in slots]
@@ -275,21 +293,10 @@
 
     each_head(attend)
 
-    def finish_sends(head):
-        q_pair(head, own_rows).wait_send()
-        kv_pair(head, own_rows).wait_send()
-        for part in range(2):
-            both_ways(lambda up: own_along(head, part, up).wait_send())
-            both_ways(lambda up: passed_along(head, part, up).wait_send())
-
-    each_head(finish_sends)
-
-    def finish(head):
-        out_keep(head).wait()
-        out_pair(head, side).wait_send()
-        out_pair(head, 1 - side).wait_recv()
-
-    each_head(finish)
+    for head in range(heads - FINISH_BEHIND, heads):
+        finish_sends(head)
+    for head in range(heads - FINISH_BEHIND, heads):
+        finish(head)
 
 
 def per_device(inner, positions, queries, key_value, region_table, region_bias):

time: 80 us -> 80 us (level)
  no operation moved by 1% of the time
where the time goes in v4:
time: 80 us; the launch traced here: 79.8 us
  Pallas kernels  77.5 us (97%)
  local copies, waits for them, and re-layouts  2.3 us (3%)
    pallas_call x1, Pallas kernels, per_device(): pl.pallas_call(functools.partial(kernel, inner, positions), out_shape=jax...  77.5 us
    unnamed x1, local copies, waits for them, and re-layouts  2.3 us

profile of v4, /device:TPU:1, one launch (start us, length us, event | category | flops | bytes accessed | tf_op | source)
XLA Modules:
  0.0 79.8 jit_solution(13158260661308237652)
XLA Ops:
  0.0 77.5 %shard_map.46 = bf16[256,2048]{1,0:T(8,128)(2,1)} custom-call(s32[8,8]{1,0:T(8,128)} %table_hbm.1, f32[16,16]{1,0:T(8,128)} %bias_hbm.1, bf16[256,2048]{1,0:T(8,128)(2,1)} %q_ref.1, bf16[2,256,2048]{2,1,0:T(8,128)(2,1)} %kv_ref.1), custom_call_target="tpu_custom_call" | custom-call | tf_op jit(solution)/shard_map/pallas_call | solution.py:309
  77.5 2.3 %copy.6 = bf16[256,2048]{1,0:T(8,128)(2,1)} copy(bf16[256,2048]{1,0:T(8,128)(2,1)} %shard_map.46) | data formatting | bytes 2097152

commit v5 on v4

--- a/solution.py
+++ b/solution.py
@@ -279,10 +279,14 @@
                 total = total + jnp.sum(weights, axis=1, keepdims=True)
                 w_buf[half, slot] = weights.astype(w_buf.dtype)
             totals.append(total)
+        started = [
+            jnp.dot(w_buf[half, OWN], kv_buf[head, OWN, 1], preferred_element_type=jnp.float32)
+            for half in range(2)
+        ]
         wait_along(head, 1)
         for half, tile in enumerate((partner_rows, own_rows)):
-            weighted = jnp.zeros((rows, head_size), jnp.float32)
-            for slot in slots:
+            weighted = started[half]
+            for slot in (BELOW, ABOVE):
                 weighted = weighted + jnp.dot(
                     w_buf[half, slot], kv_buf[head, slot, 1], preferred_element_type=jnp.float32
                 )

time: 80 us -> 80 us (level)
  no operation moved by 1% of the time
where the time goes in v5:
time: 80 us; the launch traced here: 79.8 us
  Pallas kernels  77.5 us (97%)
  local copies, waits for them, and re-layouts  2.3 us (3%)
    pallas_call x1, Pallas kernels, per_device(): pl.pallas_call(functools.partial(kernel, inner, positions), out_shape=jax...  77.5 us
    unnamed x1, local copies, waits for them, and re-layouts  2.3 us

profile of v5, /device:TPU:1, one launch (start us, length us, event | category | flops | bytes accessed | tf_op | source)
XLA Modules:
  0.0 79.8 jit_solution(13112806092546464078)
XLA Ops:
  0.0 77.5 %shard_map.46 = bf16[256,2048]{1,0:T(8,128)(2,1)} custom-call(s32[8,8]{1,0:T(8,128)} %table_hbm.1, f32[16,16]{1,0:T(8,128)} %bias_hbm.1, bf16[256,2048]{1,0:T(8,128)(2,1)} %q_ref.1, bf16[2,256,2048]{2,1,0:T(8,128)(2,1)} %kv_ref.1), custom_call_target="tpu_custom_call" | custom-call | tf_op jit(solution)/shard_map/pallas_call | solution.py:313
  77.5 2.3 %copy.6 = bf16[256,2048]{1,0:T(8,128)(2,1)} copy(bf16[256,2048]{1,0:T(8,128)(2,1)} %shard_map.46) | data formatting | bytes 2097152
